TPU v7x, 32 devices: a whole 2x2x4 slice. The times are simulated.
32 devices in a mesh: tm: 16 (over z, y, x), dp: 2 (over core).
Axes of the slice: x: 2, y: 2, z: 4, core: 2. Of those that a mesh axis runs over, the one named last changes fastest.
Arguments:
- frame_tokens: bfloat16 [2, 48, 64, 1280], P('dp', 'tm'), may hold values from -8 to 8
- visible: int32 [2, 48, 64], P('dp'), may hold values from 0 to 2
- grad_output: bfloat16 [2, 48, 64, 1280], P('dp', 'tm'), may hold values from -6 to 6
- norm_gain: float32 [1280], replicated, may hold values from 0.1 to 1.9
- query_weight: bfloat16 [1280, 640], P('tm'), may hold values from -1.5 to 1.5
- key_weight: bfloat16 [1280, 640], P('tm'), may hold values from -1.5 to 1.5
- value_weight: bfloat16 [1280, 640], P('tm'), may hold values from -0.15625 to 0.15625
- output_weight: bfloat16 [640, 1280], P('tm'), may hold values from -0.25 to 0.25
Outputs:
- block_out: bfloat16 [2, 48, 64, 1280], P('dp', 'tm')
- grad_tokens: bfloat16 [2, 48, 64, 1280], P('dp', 'tm')
- grad_output_weight: float32 [640, 1280], P('tm')
Inputs may be any that keep to these rules, and one draw needn't show every extreme that they name: visible[c, f, g] names which of the 3 cells of group g is visible in frame f.
All inputs are finite; a program needn't handle non-finite values.
Results may differ from a plain program's by a relative error of at most 0.012.
Values may be sent and summed in bfloat16 or wider, within the bound.
A program may use at most 64 MiB of HBM per device.

v0:
```python
import math

import jax
import jax.numpy as jnp
from jax import lax
from jax.sharding import PartitionSpec as P

HEADS = 8


NORM_EPS = 1e-06


def normalize(token_rows, norm_gain):
    values = token_rows.astype(jnp.float32)
    centered = values - jnp.mean(values, axis=-1, keepdims=True)
    inverse = lax.rsqrt(jnp.mean(centered * centered, axis=-1, keepdims=True) + NORM_EPS)
    scaled = centered * inverse
    return (scaled, inverse, (scaled * norm_gain).astype(jnp.bfloat16))


def project(token_rows, weight):
    lead_shape = token_rows.shape[:-1]
    flat_rows = token_rows.reshape(-1, token_rows.shape[-1])
    result = jnp.dot(flat_rows, weight, preferred_element_type=jnp.float32)
    return result.astype(jnp.bfloat16).reshape(lead_shape + (weight.shape[1],))


def split_heads(values):
    return values.reshape(values.shape[:-1] + (HEADS, values.shape[-1] // HEADS))


def attend(query_rows, key_rows, value_rows, same_cell):
    score_scale = 1.0 / math.sqrt(query_rows.shape[-1] // HEADS)
    query_heads = split_heads(query_rows)
    key_heads = split_heads(key_rows)
    value_heads = split_heads(value_rows)
    scores = (
        jnp.einsum("fghe,tghe->ghft", query_heads, key_heads, preferred_element_type=jnp.float32)
        * score_scale
    )
    scores = jnp.where(same_cell[:, None], scores, -jnp.inf)
    row_top = jnp.max(scores, axis=-1, keepdims=True)
    expons = jnp.exp(scores - row_top)
    soft_probs = expons / jnp.sum(expons, axis=-1, keepdims=True)
    probs_low = soft_probs.astype(jnp.bfloat16)
    mixed_rows = jnp.einsum(
        "ghft,tghe->fghe", probs_low, value_heads, preferred_element_type=jnp.float32
    )
    return (soft_probs, probs_low, mixed_rows.reshape(query_rows.shape).astype(jnp.bfloat16))


def attend_back(query_rows, key_rows, value_rows, soft_probs, probs_low, grad_mixed):
    score_scale = 1.0 / math.sqrt(query_rows.shape[-1] // HEADS)
    query_heads = split_heads(query_rows)
    key_heads = split_heads(key_rows)
    value_heads = split_heads(value_rows)
    grad_heads = split_heads(grad_mixed)
    grad_probs = jnp.einsum(
        "fghe,tghe->ghft", grad_heads, value_heads, preferred_element_type=jnp.float32
    )
    centre = jnp.sum(soft_probs * grad_probs, axis=-1, keepdims=True)
    grad_scores = (soft_probs * (grad_probs - centre) * score_scale).astype(jnp.bfloat16)
    grad_query = jnp.einsum(
        "ghft,tghe->fghe", grad_scores, key_heads, preferred_element_type=jnp.float32
    )
    grad_key = jnp.einsum(
        "ghft,fghe->tghe", grad_scores, query_heads, preferred_element_type=jnp.float32
    )
    grad_value = jnp.einsum(
        "ghft,fghe->tghe", probs_low, grad_heads, preferred_element_type=jnp.float32
    )
    full_shape = query_rows.shape
    return (
        grad_query.reshape(full_shape).astype(jnp.bfloat16),
        grad_key.reshape(full_shape).astype(jnp.bfloat16),
        grad_value.reshape(full_shape).astype(jnp.bfloat16),
    )


def back_project(grad_query, grad_key, grad_value, query_weight, key_weight, value_weight):
    lead_shape = grad_query.shape[:-1]
    width = grad_query.shape[-1]
    total = jnp.dot(
        grad_query.reshape(-1, width), query_weight.T, preferred_element_type=jnp.float32
    )
    total = total + jnp.dot(
        grad_key.reshape(-1, width), key_weight.T, preferred_element_type=jnp.float32
    )
    total = total + jnp.dot(
        grad_value.reshape(-1, width), value_weight.T, preferred_element_type=jnp.float32
    )
    return total.astype(jnp.bfloat16).reshape(lead_shape + (query_weight.shape[0],))


def on_device(
    frame_tokens,
    visible,
    grad_output,
    norm_gain,
    query_weight,
    key_weight,
    value_weight,
    output_weight,
):
    query_weight, key_weight, value_weight, output_weight = (
        lax.all_gather(query_weight, "tm", axis=0, tiled=True),
        lax.all_gather(key_weight, "tm", axis=0, tiled=True),
        lax.all_gather(value_weight, "tm", axis=0, tiled=True),
        lax.all_gather(output_weight, "tm", axis=0, tiled=True),
    )
    shards = lax.axis_size("tm")
    tokens = frame_tokens[0]
    frame_count, visible_count, width = tokens.shape
    att_width = output_weight.shape[0]
    groups = visible_count // shards
    scaled, inverse, normed = normalize(tokens, norm_gain)
    local_cells = lax.dynamic_slice_in_dim(visible[0], lax.axis_index("tm") * groups, groups, 1)
    cell_major = local_cells.T
    same_cell = cell_major[:, :, None] == cell_major[:, None, :]
    query_rows = project(normed, query_weight)
    key_rows = project(normed, key_weight)
    value_rows = project(normed, value_weight)
    query_rows, key_rows, value_rows = (
        lax.all_to_all(query_rows, "tm", split_axis=1, concat_axis=0, tiled=True),
        lax.all_to_all(key_rows, "tm", split_axis=1, concat_axis=0, tiled=True),
        lax.all_to_all(value_rows, "tm", split_axis=1, concat_axis=0, tiled=True),
    )
    soft_probs, probs_low, mixed_cells = attend(query_rows, key_rows, value_rows, same_cell)
    mixed_frames = lax.all_to_all(mixed_cells, "tm", split_axis=0, concat_axis=1, tiled=True)
    flat_mixed = mixed_frames.reshape(-1, att_width)
    flat_tokens = tokens.reshape(-1, width)
    update = jnp.dot(flat_mixed, output_weight, preferred_element_type=jnp.float32)
    block_rows = (
        (flat_tokens.astype(jnp.float32) + update).astype(jnp.bfloat16).reshape(tokens.shape)
    )
    flat_grad = grad_output[0].reshape(-1, width)
    grad_mixed = jnp.dot(flat_grad, output_weight.T, preferred_element_type=jnp.float32)
    grad_mixed = grad_mixed.astype(jnp.bfloat16).reshape(frame_count, visible_count, att_width)
    term_share = lax.psum_scatter(
        jnp.dot(flat_mixed.T, flat_grad, preferred_element_type=jnp.float32),
        "tm",
        scatter_dimension=0,
        tiled=True,
    )
    grad_weight = lax.psum(term_share.astype(jnp.bfloat16), "dp").astype(jnp.float32)
    grad_cells = lax.all_to_all(grad_mixed, "tm", split_axis=1, concat_axis=0, tiled=True)
    grad_query, grad_key, grad_value = attend_back(
        query_rows, key_rows, value_rows, soft_probs, probs_low, grad_cells
    )
    grad_query, grad_key, grad_value = (
        lax.all_to_all(grad_query, "tm", split_axis=0, concat_axis=1, tiled=True),
        lax.all_to_all(grad_key, "tm", split_axis=0, concat_axis=1, tiled=True),
        lax.all_to_all(grad_value, "tm", split_axis=0, concat_axis=1, tiled=True),
    )
    grad_normed = back_project(
        grad_query, grad_key, grad_value, query_weight, key_weight, value_weight
    )
    weighted = grad_normed.astype(jnp.float32) * norm_gain
    first_mean = jnp.mean(weighted, axis=-1, keepdims=True)
    second_mean = jnp.mean(weighted * scaled, axis=-1, keepdims=True)
    grad_rows = inverse * (weighted - first_mean - scaled * second_mean) + grad_output[0].astype(
        jnp.float32
    )
    return (block_rows[None], grad_rows.astype(jnp.bfloat16)[None], grad_weight)


def solution(mesh):
    return jax.shard_map(
        on_device,
        mesh=mesh,
        in_specs=(
            P("dp", "tm", None, None),
            P("dp", None, None),
            P("dp", "tm", None, None),
            P(),
            P("tm", None),
            P("tm", None),
            P("tm", None),
            P("tm", None),
        ),
        out_specs=(P("dp", "tm", None, None), P("dp", "tm", None, None), P("tm", None)),
        check_vma=False,
    )
```

profile of v0, /device:TPU:29, one launch (start us, length us, event | category | flops | bytes accessed | tf_op | source)
XLA Modules:
  0.0 370.5 jit_solution(2057940948565614668)
XLA Ops:
  7.2 0.7 all-gather.5.cloned.1.call-update
  8.0 0.7 all-gather.9.cloned.1.call-update
  10.0 1.2 convert_reduce_fusion
  11.2 1.3 fusion.21
  12.7 2.0 fusion.22
  14.7 52.2 %all-gather.5.cloned.1.call-done = bf16[1280,640]{1,0:T(8,128)(2,1)} async-done(((bf16[80,640]{1,0:T(8,128)(2,1)}), bf16[1280,640]{1,0:T(8,128)(2,1)}) %all-gather.5.cloned.1.call-update) | async-done | bytes 1638416 | tf_op jit(solution)/shard_map/all_gather | solution.py:109
  66.8 2.0 convolution_convert_fusion.7
  68.8 0.9 copy.59
  69.8 5.6 %all-to-all-start = ((bf16[3,64,640]{2,0,1:T(4,128)(2,1)}), bf16[3,64,640]{2,0,1:T(4,128)(2,1)S(1)}, u32[]{:S(2)}, u32[]{:S(2)}) async-start(bf16[3,64,640]{2,0,1:T(4,128)(2,1)} %copy.59), calls=%async_computation | async-start | bytes 655360 | tf_op jit(solution)/shard_map/all_to_all | solution.py:127
  75.4 51.8 %all-gather.9.cloned.1.call-done = bf16[1280,640]{1,0:T(8,128)(2,1)} async-done(((bf16[80,640]{1,0:T(8,128)(2,1)}), bf16[1280,640]{1,0:T(8,128)(2,1)}) %all-gather.9.cloned.1.call-update) | async-done | bytes 1638416 | tf_op jit(solution)/shard_map/all_gather | solution.py:108
  127.2 2.0 convolution_convert_fusion.5
  129.2 0.9 copy.66
  130.1 5.6 %all-to-all-start.2 = ((bf16[3,64,640]{2,0,1:T(4,128)(2,1)}), bf16[3,64,640]{2,0,1:T(4,128)(2,1)S(1)}, u32[]{:S(2)}, u32[]{:S(2)}) async-start(bf16[3,64,640]{2,0,1:T(4,128)(2,1)} %copy.66), calls=%async_computation.2 | async-start | bytes 655360 | tf_op jit(solution)/shard_map/all_to_all | solution.py:126
  135.7 51.8 %all-gather.7.cloned.1.call-done = bf16[1280,640]{1,0:T(8,128)(2,1)} async-done(((bf16[80,640]{1,0:T(8,128)(2,1)}), bf16[1280,640]{1,0:T(8,128)(2,1)}) %all-gather.7.cloned.1.call-update) | async-done | bytes 1638416 | tf_op jit(solution)/shard_map/all_gather | solution.py:107
  187.5 2.0 convolution_convert_fusion.6
  189.5 0.9 copy.63
  190.4 5.6 %all-to-all-start.1 = ((bf16[3,64,640]{2,0,1:T(4,128)(2,1)}), bf16[3,64,640]{2,0,1:T(4,128)(2,1)S(1)}, u32[]{:S(2)}, u32[]{:S(2)}) async-start(bf16[3,64,640]{2,0,1:T(4,128)(2,1)} %copy.63), calls=%async_computation.1 | async-start | bytes 655360 | tf_op jit(solution)/shard_map/all_to_all | solution.py:125
  197.5 5.7 %all-to-all-done.1 = bf16[3,64,640]{2,0,1:T(4,128)(2,1)S(1)} async-done(((bf16[3,64,640]{2,0,1:T(4,128)(2,1)}), bf16[3,64,640]{2,0,1:T(4,128)(2,1)S(1)}, u32[]{:S(2)}, u32[]{:S(2)}) %all-to-all-start.1) | async-done | bytes 245792 | tf_op jit(solution)/shard_map/all_to_all | solution.py:125
  204.1 1.1 fusion.46
  206.2 12.0 %all_to_all.120 = bf16[48,4,640]{2,1,0:T(4,128)(2,1)S(1)} all-to-all(bf16[48,4,640]{2,1,0:T(4,128)(2,1)S(1)} %reshape.161), channel_id=1, replica_groups=mesh['tm'=16,'dp'=2] {'tm'}, dimensions={0} | all-to-all | bytes 491520 | tf_op jit(solution)/shard_map/all_to_all | solution.py:130
  218.3 2.3 fusion.48
  220.7 27.6 %all-gather.11.cloned.1.call-done = bf16[640,1280]{1,0:T(8,128)(2,1)} async-done(((bf16[40,1280]{1,0:T(8,128)(2,1)}), bf16[640,1280]{1,0:T(8,128)(2,1)}) %all-gather.11.cloned.1.call-update) | async-done | bytes 1638416 | tf_op jit(solution)/shard_map/all_gather | solution.py:110
  248.3 2.1 convolution_convert_fusion.4
  250.6 14.2 %all_to_all.121 = bf16[3,64,640]{2,0,1:T(4,128)(2,1)S(1)} all-to-all(bf16[3,64,640]{2,0,1:T(4,128)(2,1)S(1)} %copy.76), channel_id=1, replica_groups=mesh['tm'=16,'dp'=2] {'tm'}, dimensions={1} | all-to-all | bytes 491520 | tf_op jit(solution)/shard_map/all_to_all | solution.py:147
  265.4 1.3 fusion.32
  266.7 2.4 fusion.13
  269.2 1.1 reshape.162
  270.3 7.3 %all-to-all-start.5 = ((bf16[48,4,640]{2,1,0:T(4,128)(2,1)}), bf16[48,4,640]{2,1,0:T(4,128)(2,1)S(1)}, u32[]{:S(2)}, u32[]{:S(2)}) async-start(bf16[48,4,640]{2,1,0:T(4,128)(2,1)} %reshape.162), calls=%async_computation.5 | async-start | bytes 491520 | tf_op jit(solution)/shard_map/all_to_all | solution.py:152
  277.6 2.4 fusion.14
  280.1 1.1 reshape.163
  281.2 3.9 %all-to-all-done.5 = bf16[48,4,640]{2,1,0:T(4,128)(2,1)S(1)} async-done(((bf16[48,4,640]{2,1,0:T(4,128)(2,1)}), bf16[48,4,640]{2,1,0:T(4,128)(2,1)S(1)}, u32[]{:S(2)}, u32[]{:S(2)}) %all-to-all-start.5) | async-done | bytes 245792 | tf_op jit(solution)/shard_map/all_to_all | solution.py:152
  285.1 8.6 %all-to-all-start.6 = ((bf16[48,4,640]{2,1,0:T(4,128)(2,1)}), bf16[48,4,640]{2,1,0:T(4,128)(2,1)S(1)}, u32[]{:S(2)}, u32[]{:S(2)}) async-start(bf16[48,4,640]{2,1,0:T(4,128)(2,1)} %reshape.163), calls=%async_computation.6 | async-start | bytes 491520 | tf_op jit(solution)/shard_map/all_to_all | solution.py:153
  293.7 1.8 fusion.15
  295.6 1.1 reshape.164
  296.7 5.0 %all-to-all-done.6 = bf16[48,4,640]{2,1,0:T(4,128)(2,1)S(1)} async-done(((bf16[48,4,640]{2,1,0:T(4,128)(2,1)}), bf16[48,4,640]{2,1,0:T(4,128)(2,1)S(1)}, u32[]{:S(2)}, u32[]{:S(2)}) %all-to-all-start.6) | async-done | bytes 245792 | tf_op jit(solution)/shard_map/all_to_all | solution.py:153
  301.7 8.6 %all-to-all-start.7 = ((bf16[48,4,640]{2,1,0:T(4,128)(2,1)}), bf16[48,4,640]{2,1,0:T(4,128)(2,1)S(1)}, u32[]{:S(2)}, u32[]{:S(2)}) async-start(bf16[48,4,640]{2,1,0:T(4,128)(2,1)} %reshape.164), calls=%async_computation.7 | async-start | bytes 491520 | tf_op jit(solution)/shard_map/all_to_all | solution.py:154
  310.4 0.8 reshape.156
  311.2 0.8 reshape.157
  312.0 6.2 %all-to-all-done.7 = bf16[48,4,640]{2,1,0:T(4,128)(2,1)S(1)} async-done(((bf16[48,4,640]{2,1,0:T(4,128)(2,1)}), bf16[48,4,640]{2,1,0:T(4,128)(2,1)S(1)}, u32[]{:S(2)}, u32[]{:S(2)}) %all-to-all-start.7) | async-done | bytes 245792 | tf_op jit(solution)/shard_map/all_to_all | solution.py:154
  318.3 2.3 fusion.47
  321.4 0.7 copy-done.3
  322.4 1.7 multiply_reduce_fusion.2
  324.3 2.6 fusion.28
  326.8 10.2 %reduce-scatter.2.cloned.1.call-done = f32[40,1280]{1,0:T(8,128)} async-done(((f32[640,1280]{1,0:T(8,128)}), f32[40,1280]{1,0:T(8,128)}) %reduce-scatter.2.cloned.1.call-update) | async-done | bytes 204816 | tf_op jit(solution)/shard_map/reduce_scatter | solution.py:140
  337.1 1.6 convert_element_type.140
  338.7 1.3 fusion.2
  340.0 22.0 %all-reduce.2.cloned.1.call-done = bf16[40,1280]{1,0:T(8,128)(2,1)} async-done(((bf16[40,1280]{1,0:T(8,128)(2,1)}), bf16[40,1280]{1,0:T(8,128)(2,1)}) %all-reduce.2.cloned.1.call-update) | async-done | bytes 102416 | tf_op jit(solution)/shard_map/psum | solution.py:146
  362.0 1.6 convert_element_type.141
  (64 shorter events, 7.5 us)
Async XLA Ops:
  7.2 188.9 %copy-start = (s32[1,48,64]{2,1,0:T(8,128)S(1)}, s32[1,48,64]{2,1,0:T(8,128)}, u32[]{:S(2)}) copy-start(s32[1,48,64]{2,1,0:T(8,128)} %param.9) | copy-start | bytes 36868
  7.2 5.5 %copy-start.1 = (bf16[1,3,64,1280]{3,2,1,0:T(8,128)(2,1)S(1)}, bf16[1,3,64,1280]{3,2,1,0:T(8,128)(2,1)}, u32[]{:S(2)}) copy-start(bf16[1,3,64,1280]{3,2,1,0:T(8,128)(2,1)} %param.8) | copy-start | bytes 1474564
  7.2 59.6 %all-gather.5.cloned.1.call-start = ((), (), s32[]{:S(2)}) async-start(), calls=%async_computation.9 | async-start | bytes 1740800 | tf_op jit(solution)/shard_map/all_gather | solution.py:109
  7.9 119.2 %all-gather.9.cloned.1.call-start = ((), (), s32[]{:S(2)}) async-start(), calls=%async_computation.11 | async-start | bytes 1740800 | tf_op jit(solution)/shard_map/all_gather | solution.py:108
  8.7 178.8 %all-gather.7.cloned.1.call-start = ((), (), s32[]{:S(2)}) async-start(), calls=%async_computation.10 | async-start | bytes 1740800 | tf_op jit(solution)/shard_map/all_gather | solution.py:107
  9.4 238.9 %all-gather.11.cloned.1.call-start = ((), (), s32[]{:S(2)}) async-start(), calls=%async_computation.12 | async-start | bytes 1740800 | tf_op jit(solution)/shard_map/all_gather | solution.py:110
  69.8 60.3 %all-to-all-start = ((bf16[3,64,640]{2,0,1:T(4,128)(2,1)}), bf16[3,64,640]{2,0,1:T(4,128)(2,1)S(1)}, u32[]{:S(2)}, u32[]{:S(2)}) async-start(bf16[3,64,640]{2,0,1:T(4,128)(2,1)} %copy.59), calls=%async_computation | async-start | bytes 655360 | tf_op jit(solution)/shard_map/all_to_all | solution.py:127
  130.1 60.3 %all-to-all-start.2 = ((bf16[3,64,640]{2,0,1:T(4,128)(2,1)}), bf16[3,64,640]{2,0,1:T(4,128)(2,1)S(1)}, u32[]{:S(2)}, u32[]{:S(2)}) async-start(bf16[3,64,640]{2,0,1:T(4,128)(2,1)} %copy.66), calls=%async_computation.2 | async-start | bytes 655360 | tf_op jit(solution)/shard_map/all_to_all | solution.py:126
  190.4 12.7 %all-to-all-start.1 = ((bf16[3,64,640]{2,0,1:T(4,128)(2,1)}), bf16[3,64,640]{2,0,1:T(4,128)(2,1)S(1)}, u32[]{:S(2)}, u32[]{:S(2)}) async-start(bf16[3,64,640]{2,0,1:T(4,128)(2,1)} %copy.63), calls=%async_computation.1 | async-start | bytes 655360 | tf_op jit(solution)/shard_map/all_to_all | solution.py:125
  196.0 141.0 %reduce-scatter.2.cloned.1.call-start = ((), (), s32[]{:S(2)}) async-start(), calls=%async_computation.13 | async-start | bytes 3481600 | tf_op jit(solution)/shard_map/reduce_scatter | solution.py:140
  204.1 1.1 copy-start.8
  205.6 12.7 %copy-start.5 = (bf16[1,3,64,1280]{3,2,1,0:T(8,128)(2,1)S(1)}, bf16[1,3,64,1280]{3,2,1,0:T(8,128)(2,1)}, u32[]{:S(2)}) copy-start(bf16[1,3,64,1280]{3,2,1,0:T(8,128)(2,1)} %param.10) | copy-start | bytes 1474564
  270.3 14.8 %all-to-all-start.5 = ((bf16[48,4,640]{2,1,0:T(4,128)(2,1)}), bf16[48,4,640]{2,1,0:T(4,128)(2,1)S(1)}, u32[]{:S(2)}, u32[]{:S(2)}) async-start(bf16[48,4,640]{2,1,0:T(4,128)(2,1)} %reshape.162), calls=%async_computation.5 | async-start | bytes 491520 | tf_op jit(solution)/shard_map/all_to_all | solution.py:152
  285.1 16.6 %all-to-all-start.6 = ((bf16[48,4,640]{2,1,0:T(4,128)(2,1)}), bf16[48,4,640]{2,1,0:T(4,128)(2,1)S(1)}, u32[]{:S(2)}, u32[]{:S(2)}) async-start(bf16[48,4,640]{2,1,0:T(4,128)(2,1)} %reshape.163), calls=%async_computation.6 | async-start | bytes 491520 | tf_op jit(solution)/shard_map/all_to_all | solution.py:153
  301.7 16.4 %all-to-all-start.7 = ((bf16[48,4,640]{2,1,0:T(4,128)(2,1)}), bf16[48,4,640]{2,1,0:T(4,128)(2,1)S(1)}, u32[]{:S(2)}, u32[]{:S(2)}) async-start(bf16[48,4,640]{2,1,0:T(4,128)(2,1)} %reshape.164), calls=%async_computation.7 | async-start | bytes 491520 | tf_op jit(solution)/shard_map/all_to_all | solution.py:154
  310.3 51.8 %all-reduce.2.cloned.1.call-start = ((), (), s32[]{:S(2)}) async-start(), calls=%async_computation.14 | async-start | bytes 204800 | tf_op jit(solution)/shard_map/psum | solution.py:146
  318.2 2.4 copy-start.4
  318.3 2.4 copy-start.7
  320.7 1.4 copy-start.3
  320.7 1.7 copy-start.6
  320.7 1.7 copy-start.9
  324.1 14.6 %copy-start.2 = (bf16[640,1280]{1,0:T(8,128)(2,1)S(1)}, bf16[640,1280]{1,0:T(8,128)(2,1)}, u32[]{:S(2)}) copy-start(bf16[640,1280]{1,0:T(8,128)(2,1)} %all-gather.11.cloned.1.call-done) | copy-start | bytes 4915204
Sparse Core Ops, SparseCore 0:
  10.7 56.0 all-gather.4
  69.5 57.5 all-gather.8
  129.9 57.5 all-gather.6
  190.0 58.1 all-gather.10
  250.4 86.6 reduce-scatter.1
  339.8 22.1 all-reduce.1
where the time goes:
time: 373 us; the launch traced here: 370 us
  waiting for transfers between devices  239 us (64%)
  starting transfers between devices  41.5 us (11%)
  blocking collectives  26.2 us (7%)
  matrix products  25.2 us (7%)
  between operations  14.5 us (4%)
  local copies, waits for them, and re-layouts  12.8 us (3%)
  other arithmetic  11.5 us (3%)
    all_gather x1, waiting for transfers between devices, on_device(): lax.all_gather(value_weight, 'tm', axis=0, tiled=True)  52.2 us
    all_gather x1, waiting for transfers between devices, on_device(): lax.all_gather(query_weight, 'tm', axis=0, tiled=True)  51.8 us
    all_gather x1, waiting for transfers between devices, on_device(): lax.all_gather(key_weight, 'tm', axis=0, tiled=True)  51.8 us
    all_gather x1, waiting for transfers between devices, on_device(): lax.all_gather(output_weight, 'tm', axis=0, tiled=True)  27.6 us
    psum x1, waiting for transfers between devices, on_device(): lax.psum(term_share.astype(jnp.bfloat16), 'dp').astype(jnp.float32)  22 us
    all_to_all x1, blocking collectives, on_device(): lax.all_to_all(grad_mixed, 'tm', split_axis=1, concat_axis=0, tiled=True)  14.2 us
    all_to_all x1, blocking collectives, on_device(): lax.all_to_all(mixed_cells, 'tm', split_axis=0, concat_axis=1, tiled=True)  12 us
    reduce_scatter x1, waiting for transfers between devices, on_device(): lax.psum_scatter(jnp.dot(flat_mixed.T, flat_grad, preferred_element_type=...  10.2 us
  transfers between devices with their start and end apart: 12, of which 10 were waited for; matrix products, arithmetic and copies ran while one was open for 12% of the time, Pallas kernels for 0%

commit v1 on v0

--- a/solution.py
+++ b/solution.py
@@ -3,6 +3,8 @@
 import jax
 import jax.numpy as jnp
 from jax import lax
+from jax.experimental import pallas as pl
+from jax.experimental.pallas import tpu as pltpu
 from jax.sharding import PartitionSpec as P
 
 HEADS = 8
@@ -165,9 +167,413 @@
     return (block_rows[None], grad_rows.astype(jnp.bfloat16)[None], grad_weight)
 
 
+SHARDS = 16
+ROWS = 16
+
+
+def nt_dot(left, right):
+    return lax.dot_general(left, right, (((1,), (1,)), ((), ())), preferred_element_type=jnp.float32)
+
+
+def tn_dot(left, right):
+    return lax.dot_general(left, right, (((0,), (0,)), ((), ())), preferred_element_type=jnp.float32)
+
+
+def nn_dot(left, right):
+    return jnp.dot(left, right, preferred_element_type=jnp.float32)
+
+
+def head_window(head, head_dim):
+    low = head * head_dim
+    start = low // 128 * 128
+    stop = -(-(low + head_dim) // 128) * 128
+    lane = lax.broadcasted_iota(jnp.int32, (1, stop - start), 1) + start
+    inside = jnp.where((lane >= low) & (lane < low + head_dim), 1.0, 0.0)
+    return (slice(start, stop), inside.astype(jnp.bfloat16))
+
+
+def fused_kernel(
+    tok, gout, gain, code_col, code_row, w4,
+    block_o, gtok_o, dw_o,
+    wall, norm_s, norm_r, gout_r, q_s, k_s, v_s, gm_s, probs_s,
+    acc_a, acc_b, acc_c, mix_s, mix_r, gn_s, gn_r,
+    dwp, dw_in, dwc_s, dwc_r, dwf,
+    w_send, w_recv, sib_send, sib_recv, go_send, go_recv, no_send, no_recv,
+    mi_send, mi_recv, gn_send, gn_recv, dw_send, dw_recv, pair_send, pair_recv,
+):
+    t = lax.axis_index("tm")
+    c = lax.axis_index("dp")
+    x = lax.rem(t, 2)
+    y = lax.rem(lax.div(t, 2), 2)
+    z = lax.div(t, 4)
+    plane = lax.rem(t, 4)
+    xn = t + 1 - 2 * x
+    yn = t + 2 - 4 * y
+    att = q_s.shape[1]
+    head_dim = att // HEADS
+    scale = 1.0 / math.sqrt(head_dim)
+    half = pl.ds(2 * c, 2)
+
+    def to_tm(src, dst, send, recv, peer):
+        return pltpu.make_async_remote_copy(
+            src_ref=src, dst_ref=dst, send_sem=send, recv_sem=recv,
+            device_id={"tm": peer}, device_id_type=pl.DeviceIdType.MESH,
+        )
+
+    def to_pair(src, dst, send, recv):
+        return pltpu.make_async_remote_copy(
+            src_ref=src, dst_ref=dst, send_sem=send, recv_sem=recv,
+            device_id={"dp": 1 - c}, device_id_type=pl.DeviceIdType.MESH,
+        )
+
+    barrier = pltpu.get_barrier_semaphore()
+
+    @pl.loop(1, SHARDS)
+    def _(d):
+        pl.semaphore_signal(
+            barrier, inc=1, device_id={"tm": lax.rem(t + d, SHARDS)},
+            device_id_type=pl.DeviceIdType.MESH,
+        )
+
+    pl.semaphore_signal(
+        barrier, inc=1, device_id={"dp": 1 - c}, device_id_type=pl.DeviceIdType.MESH
+    )
+    pl.semaphore_wait(barrier, SHARDS)
+
+    def item(s):
+        return wall.at[half, s]
+
+    def own_item(peer, slot):
+        return to_tm(w4.at[half], item(t), w_send.at[slot], w_recv.at[t], peer)
+
+    for slot, peer in ((3, xn), (7, yn)):
+        own_item(peer, slot).start()
+    for i in range(1, 4):
+        own_item(lax.rem(z + i, 4) * 4 + plane, i - 1).start()
+
+    def peer_copy(src, dst, send, recv, peer):
+        return to_tm(src.at[peer], dst.at[t], send.at[peer], recv.at[t], peer)
+
+    def wait_peers(src, dst, send, recv, sends):
+        @pl.loop(1, SHARDS)
+        def _(d):
+            peer = lax.rem(t + d, SHARDS)
+            if sends:
+                peer_copy(src, dst, send, recv, peer).wait_send()
+            else:
+                to_tm(src.at[peer], dst.at[peer], send.at[peer], recv.at[peer], peer).wait_recv()
+
+    @pl.loop(1, SHARDS)
+    def _(d):
+        peer_copy(gout, gout_r, go_send, go_recv, lax.rem(t + d, SHARDS)).start()
+
+    def norm_block(p):
+        values = tok[p].astype(jnp.float32)
+        centered = values - jnp.mean(values, axis=-1, keepdims=True)
+        inverse = lax.rsqrt(jnp.mean(centered * centered, axis=-1, keepdims=True) + NORM_EPS)
+        return (centered * inverse, inverse)
+
+    @pl.loop(1, SHARDS + 1)
+    def _(d):
+        peer = lax.rem(t + d, SHARDS)
+        norm_s[peer] = (norm_block(peer)[0] * gain[...]).astype(jnp.bfloat16)
+
+        @pl.when(d < SHARDS)
+        def _():
+            peer_copy(norm_s, norm_r, no_send, no_recv, peer).start()
+
+    norm_r[t] = norm_s[t]
+    gout_r[t] = gout[t]
+    for j in range(4):
+        wall[j, t] = w4[j]
+
+    def wait_item(s):
+        to_tm(item(s), item(s), w_send.at[0], w_recv.at[s], xn).wait_recv()
+
+    def pass_item(s, peer, slot):
+        return to_tm(item(s), item(s), w_send.at[slot], w_recv.at[s], peer)
+
+    def pair_item(s):
+        return to_pair(item(s), item(s), sib_send.at[s], sib_recv.at[s])
+
+    for i in range(4):
+        level = lax.rem(z + 4 - i, 4) * 4
+        mine = level + plane
+        if i > 0:
+            wait_item(mine)
+            pass_item(mine, xn, 3 + i).start()
+            pass_item(mine, yn, 7 + i).start()
+            pair_item(mine).start()
+    for i in range(4):
+        level = lax.rem(z + 4 - i, 4) * 4
+        from_x = level + lax.rem(xn, 4)
+        from_y = level + lax.rem(yn, 4)
+
+        wait_item(from_x)
+
+        @pl.when(c == 0)
+        def _():
+            pass_item(from_x, yn, 11 + i).start()
+
+        pair_item(from_x).start()
+        wait_item(from_y)
+
+        @pl.when(c == 1)
+        def _():
+            pass_item(from_y, xn, 11 + i).start()
+
+        pair_item(from_y).start()
+    for i in range(4):
+        level = lax.rem(z + 4 - i, 4) * 4
+        across = level + 3 - plane
+        wait_item(across)
+        pair_item(across).start()
+
+    wait_peers(norm_s, norm_r, no_send, no_recv, False)
+    wait_peers(gout, gout_r, go_send, go_recv, False)
+
+    other = pl.ds(2 - 2 * c, 2)
+
+    @pl.loop(1, SHARDS)
+    def _(d):
+        s = lax.rem(t + d, SHARDS)
+        to_pair(
+            wall.at[other, s], wall.at[other, s], sib_send.at[s], sib_recv.at[s]
+        ).wait_recv()
+
+    width = tok.shape[2]
+    depth = w4.shape[1]
+    rows = SHARDS * ROWS
+
+    def full(j):
+        return wall[j].reshape(SHARDS * depth, att)
+
+    share = depth // 2
+
+    def output_half(j):
+        blocks = wall[3].astype(jnp.float32)[:, j * share : (j + 1) * share]
+        return blocks.reshape(SHARDS * share, att).astype(jnp.bfloat16)
+
+    normed = norm_r[...].reshape(rows, width)
+    grads = gout_r[...].reshape(rows, width)
+    q_s[...] = nn_dot(normed, full(0)).astype(jnp.bfloat16)
+    k_s[...] = nn_dot(normed, full(1)).astype(jnp.bfloat16)
+    v_s[...] = nn_dot(normed, full(2)).astype(jnp.bfloat16)
+
+    same = code_col[...] == code_row[...]
+    acc_a[...] = jnp.zeros_like(acc_a)
+    for head in range(HEADS):
+        window, inside = head_window(head, head_dim)
+        scores = nt_dot(q_s[:, window] * inside, k_s[:, window]) * scale
+        scores = jnp.where(same, scores, -jnp.inf)
+        expons = jnp.exp(scores - jnp.max(scores, axis=-1, keepdims=True))
+        probs = expons / jnp.sum(expons, axis=-1, keepdims=True)
+        probs_s[head] = probs
+        acc_a[:, window] += nn_dot(probs.astype(jnp.bfloat16), v_s[:, window] * inside)
+    mix_s[...] = acc_a[...].astype(jnp.bfloat16).reshape(SHARDS, ROWS, att)
+
+    @pl.loop(1, SHARDS)
+    def _(d):
+        peer_copy(mix_s, mix_r, mi_send, mi_recv, lax.rem(t + d, SHARDS)).start()
+
+    mix_r[t] = mix_s[t]
+
+    mixed = mix_s[...].reshape(rows, att)
+    for j in range(2):
+        term = tn_dot(mixed, grads[:, j * att : (j + 1) * att])
+        dwp[j] = term.reshape(SHARDS, share, att).astype(jnp.bfloat16)
+    pair_term = to_pair(dwp.at[1 - c], dw_in, pair_send.at[0], pair_recv.at[0])
+    pair_term.start()
+
+    gm_s[:, :] = (
+        nt_dot(grads[:, :att], output_half(0)) + nt_dot(grads[:, att:], output_half(1))
+    ).astype(jnp.bfloat16)
+
+    pair_term.wait_recv()
+
+    @pl.loop(1, SHARDS + 1)
+    def _(d):
+        peer = lax.rem(t + d, SHARDS)
+        total = dwp[c, peer].astype(jnp.float32) + dw_in[peer].astype(jnp.float32)
+        dwc_s[peer] = total.astype(jnp.bfloat16)
+
+        @pl.when(d < SHARDS)
+        def _():
+            peer_copy(dwc_s, dwc_r, dw_send, dw_recv, peer).start()
+
+    dwc_r[t] = dwc_s[t]
+
+    acc_a[...] = jnp.zeros_like(acc_a)
+    acc_b[...] = jnp.zeros_like(acc_b)
+    acc_c[...] = jnp.zeros_like(acc_c)
+    for head in range(HEADS):
+        window, inside = head_window(head, head_dim)
+        grad_head = gm_s[:, window] * inside
+        probs = probs_s[head]
+        grad_probs = nt_dot(grad_head, v_s[:, window])
+        centre = jnp.sum(probs * grad_probs, axis=-1, keepdims=True)
+        grad_scores = (probs * (grad_probs - centre) * scale).astype(jnp.bfloat16)
+        acc_a[:, window] += nn_dot(grad_scores, k_s[:, window] * inside)
+        acc_b[:, window] += tn_dot(grad_scores, q_s[:, window] * inside)
+        acc_c[:, window] += tn_dot(probs.astype(jnp.bfloat16), grad_head)
+    total = nt_dot(acc_a[...].astype(jnp.bfloat16), full(0))
+    total += nt_dot(acc_b[...].astype(jnp.bfloat16), full(1))
+    total += nt_dot(acc_c[...].astype(jnp.bfloat16), full(2))
+    gn_s[...] = total.astype(jnp.bfloat16).reshape(SHARDS, ROWS, width)
+
+    @pl.loop(1, SHARDS)
+    def _(d):
+        peer_copy(gn_s, gn_r, gn_send, gn_recv, lax.rem(t + d, SHARDS)).start()
+
+    gn_r[t] = gn_s[t]
+
+    wait_peers(mix_s, mix_r, mi_send, mi_recv, False)
+    mixed_frames = mix_r[...].reshape(rows, att)
+    for j in range(2):
+        columns = slice(j * att, (j + 1) * att)
+        update = nn_dot(mixed_frames, output_half(j)).reshape(SHARDS, ROWS, att)
+        block_o[:, :, columns] = (tok[:, :, columns].astype(jnp.float32) + update).astype(
+            jnp.bfloat16
+        )
+
+    wait_peers(dwc_s, dwc_r, dw_send, dw_recv, False)
+    dwf[c] = jnp.sum(dwc_r[...].astype(jnp.float32), axis=0)
+    pair_sum = to_pair(dwf.at[c], dwf.at[c], pair_send.at[1], pair_recv.at[1])
+    pair_sum.start()
+
+    wait_peers(gn_s, gn_r, gn_send, gn_recv, False)
+
+    @pl.loop(0, SHARDS)
+    def _(p):
+        scaled, inverse = norm_block(p)
+        weighted = gn_r[p].astype(jnp.float32) * gain[...]
+        first = jnp.mean(weighted, axis=-1, keepdims=True)
+        second = jnp.mean(weighted * scaled, axis=-1, keepdims=True)
+        result = inverse * (weighted - first - scaled * second) + gout[p].astype(jnp.float32)
+        gtok_o[p] = result.astype(jnp.bfloat16)
+
+    to_pair(dwf.at[1 - c], dwf.at[1 - c], pair_send.at[1], pair_recv.at[1]).wait_recv()
+    dw_o[...] = dwf[...]
+
+    pair_term.wait_send()
+    pair_sum.wait_send()
+    for slot in range(15):
+        pass_item(t, xn, slot).wait_send()
+
+    @pl.loop(1, SHARDS)
+    def _(d):
+        pair_item(lax.rem(t + d, SHARDS)).wait_send()
+
+    wait_peers(gout, gout_r, go_send, go_recv, True)
+    wait_peers(norm_s, norm_r, no_send, no_recv, True)
+    wait_peers(mix_s, mix_r, mi_send, mi_recv, True)
+    wait_peers(dwc_s, dwc_r, dw_send, dw_recv, True)
+    wait_peers(gn_s, gn_r, gn_send, gn_recv, True)
+
+
+def to_blocks(rows):
+    frames, cells, width = rows.shape
+    groups = cells // SHARDS
+    blocks = rows.reshape(frames, SHARDS, groups, width).transpose(1, 0, 2, 3)
+    blocks = blocks.reshape(SHARDS, frames * groups, width)
+    return jnp.pad(blocks, ((0, 0), (0, ROWS - frames * groups), (0, 0)))
+
+
+def from_blocks(blocks, shape):
+    frames, cells, width = shape
+    groups = cells // SHARDS
+    rows = blocks[:, : frames * groups].reshape(SHARDS, frames, groups, width)
+    return rows.transpose(1, 0, 2, 3).reshape(shape)
+
+
+def on_chip_grid(
+    frame_tokens,
+    visible,
+    grad_output,
+    norm_gain,
+    query_weight,
+    key_weight,
+    value_weight,
+    output_weight,
+):
+    tokens = frame_tokens[0]
+    frames, cells, width = tokens.shape
+    groups = cells // SHARDS
+    depth, att = query_weight.shape
+    share = output_weight.shape[0]
+    local = lax.dynamic_slice_in_dim(visible[0], lax.axis_index("tm") * groups, groups, 1)
+    codes = local + 4 * jnp.arange(groups, dtype=jnp.int32)[None]
+    codes = jnp.pad(
+        codes.reshape(SHARDS, frames * groups),
+        ((0, 0), (0, ROWS - frames * groups)),
+        constant_values=-1,
+    )
+    output_rows = jnp.concatenate([output_weight[:, :att], output_weight[:, att:]], axis=0)
+    stacked = jnp.stack([query_weight, key_weight, value_weight, output_rows])
+    rows = SHARDS * ROWS
+    low, high = jnp.bfloat16, jnp.float32
+    vmem = pl.BlockSpec(memory_space=pltpu.VMEM)
+    dma = pltpu.SemaphoreType.DMA
+    block_rows, grad_rows, grad_weight = pl.pallas_call(
+        fused_kernel,
+        out_shape=(
+            jax.ShapeDtypeStruct((SHARDS, ROWS, width), low),
+            jax.ShapeDtypeStruct((SHARDS, ROWS, width), low),
+            jax.ShapeDtypeStruct((2, share, att), high),
+        ),
+        in_specs=[vmem] * 6,
+        out_specs=(vmem,) * 3,
+        scratch_shapes=[
+            pltpu.VMEM((4, SHARDS, depth, att), low),
+            pltpu.VMEM((SHARDS, ROWS, width), low),
+            pltpu.VMEM((SHARDS, ROWS, width), low),
+            pltpu.VMEM((SHARDS, ROWS, width), low),
+            pltpu.VMEM((rows, att), low),
+            pltpu.VMEM((rows, att), low),
+            pltpu.VMEM((rows, att), low),
+            pltpu.VMEM((rows, att), low),
+            pltpu.VMEM((HEADS, rows, rows), high),
+            pltpu.VMEM((rows, att), high),
+            pltpu.VMEM((rows, att), high),
+            pltpu.VMEM((rows, att), high),
+            pltpu.VMEM((SHARDS, ROWS, att), low),
+            pltpu.VMEM((SHARDS, ROWS, att), low),
+            pltpu.VMEM((SHARDS, ROWS, width), low),
+            pltpu.VMEM((SHARDS, ROWS, width), low),
+            pltpu.VMEM((2, SHARDS, share, att), low),
+            pltpu.VMEM((SHARDS, share, att), low),
+            pltpu.VMEM((SHARDS, share, att), low),
+            pltpu.VMEM((SHARDS, share, att), low),
+            pltpu.VMEM((2, share, att), high),
+            dma((15,)),
+            *[dma((SHARDS,))] * 13,
+            dma((2,)),
+            dma((2,)),
+        ],
+        compiler_params=pltpu.CompilerParams(
+            collective_id=0, has_side_effects=True, vmem_limit_bytes=56 * 1024 * 1024
+        ),
+        name="temporal_block",
+    )(
+        to_blocks(tokens),
+        to_blocks(grad_output[0]),
+        norm_gain[None],
+        codes.reshape(rows, 1),
+        codes.reshape(1, rows),
+        stacked,
+    )
+    grad_weight = jnp.concatenate([grad_weight[0], grad_weight[1]], axis=1)
+    return (
+        from_blocks(block_rows, tokens.shape)[None],
+        from_blocks(grad_rows, tokens.shape)[None],
+        grad_weight,
+    )
+
+
 def solution(mesh):
+    chip_grid = mesh.shape["tm"] == SHARDS and mesh.shape["dp"] == 2
     return jax.shard_map(
-        on_device,
+        on_chip_grid if chip_grid else on_device,
         mesh=mesh,
         in_specs=(
             P("dp", "tm", None, None),

time: 373 us -> 119 us (0.32)
  waiting for transfers between devices: 239 us -> 0 us
  Pallas kernels: 0 us -> 105 us
  starting transfers between devices: 41.5 us -> 0 us
  blocking collectives: 26.2 us -> 0 us
  matrix products: 25.2 us -> 0 us
  between operations: 14.5 us -> 0.81 us
  other arithmetic: 11.5 us -> 1.53 us
    all_gather x4 -> x0, waiting for transfers between devices: 183 us -> none  [the longest x1 52.2 us: on_device(): lax.all_gather(value_weight, 'tm', axis=0, tiled=True)]
    pallas_call x0 -> x1, Pallas kernels: none -> 105 us  [on_chip_grid(): pl.pallas_call(fused_kernel, out_shape=(jax.ShapeDtypeStruct((SHARDS, ROW...]
    all_to_all x6 -> x0, starting transfers between devices: 41.3 us -> none  [the longest x1 8.63 us: on_device(): lax.all_to_all(grad_key, 'tm', split_axis=0, concat_axis=1, tiled=True)]
    all_to_all x2 -> x0, blocking collectives: 26.2 us -> none  [the longest x1 14.2 us: on_device(): lax.all_to_all(grad_mixed, 'tm', split_axis=1, concat_axis=0, tiled=True)]
    dot_general x15 -> x0, matrix products: 25.2 us -> none  [the longest x3 5.95 us: project(): result = jnp.dot(flat_rows, weight, preferred_element_type=jnp.float32)]
    psum x1 -> x0, waiting for transfers between devices: 22 us -> none  [on_device(): lax.psum(term_share.astype(jnp.bfloat16), 'dp').astype(jnp.float32)]
    all_to_all x6 -> x0, waiting for transfers between devices: 20.7 us -> none  [the longest x1 6.15 us: on_device(): lax.all_to_all(grad_value, 'tm', split_axis=0, concat_axis=1, tiled=True)]
    reduce_scatter x1 -> x0, waiting for transfers between devices: 10.2 us -> none  [on_device(): lax.psum_scatter(jnp.dot(flat_mixed.T, flat_grad, preferred_element_type=...]
  transfers between devices with their start and end apart: 12 -> 0, of which waited for: 10 -> 0; matrix products, arithmetic and copies ran while one was open for 12% -> 0% of each run, Pallas kernels for 0% -> 0%
where the time goes in v1:
time: 119 us; the launch traced here: 117 us
  Pallas kernels  105 us (88%)
  local copies, waits for them, and re-layouts  9.91 us (8%)
  other arithmetic  1.53 us (1%)
    pallas_call x1, Pallas kernels, on_chip_grid(): pl.pallas_call(fused_kernel, out_shape=(jax.ShapeDtypeStruct((SHARDS, ROW...  105 us

profile of v1, /device:TPU:29, one launch (start us, length us, event | category | flops | bytes accessed | tf_op | source)
XLA Modules:
  0.0 117.3 jit_solution(9130115487807030301)
XLA Ops:
  0.6 0.0 copy-start
  0.6 0.0 copy-start.8
  0.7 0.1 add.24
  0.8 1.3 %broadcast_in_dim.4.gain = f32[1,1280]{1,0:T(1,128)} reshape(f32[1280]{0:T(1024)} %param.11) | data formatting | bytes 10240 | tf_op jit(solution)/shard_map/broadcast_in_dim | solution.py:560
  2.1 0.0 copy-done
  2.1 0.1 constant_dynamic-slice_fusion
  2.1 0.1 dynamic_slice.6
  2.2 0.6 reshape.36.code_row
  2.9 0.0 copy-done.8
  2.9 0.0 copy-start.5
  2.9 0.0 copy-start.6
  2.9 0.0 copy-start.7
  2.9 0.0 copy-start.2
  2.9 0.8 reshape.39.code_col
  3.7 0.1 copy-done.5
  3.8 0.1 copy-done.6
  3.8 0.1 copy-done.7
  3.9 0.8 pad_maximum_fusion.w4
  4.7 0.0 copy-done.2
  4.7 0.1 reshape_squeeze.6
  4.8 0.1 copy.20
  4.9 0.2 copy.21
  5.0 0.0 copy-start.3
  5.0 0.9 pad.11.tok
  5.9 0.3 copy-done.3
  6.2 0.1 reshape_squeeze.7
  6.3 0.1 copy.22
  6.4 0.2 copy.23
  6.5 0.9 pad.12.gout
  7.5 105.1 %temporal_block.1 = (bf16[16,16,1280]{2,1,0:T(8,128)(2,1)}, bf16[16,16,1280]{2,1,0:T(8,128)(2,1)}, f32[2,40,640]{2,1,0:T(8,128)}) custom-call(bf16[16,16,1280]{2,1,0:T(8,128)(2,1)} %pad.11.tok, bf16[16,16,1280]{2,1,0:T(8,128)(2,1)} %pad.12.gout, f32[1,1280]{1,0:T(1,128)} %broadcast_in_dim.4.gain, s32[256,1]{1,0:T(8,128)} %reshape.39.code_col, ...), custom_call_target="tpu_custom_call" | custom-call | tf_op jit(solution)/shard_map/temporal_block/pallas_call | solution.py:517
  112.5 1.2 %copy.25 = bf16[16,12,1280]{2,0,1:T(8,128)(2,1)S(1)} copy(bf16[16,12,1280]{2,1,0:T(8,128)(2,1)} %bitcast.32) | data formatting | bytes 983040 | tf_op jit(solution)/shard_map/slice | solution.py:485
  113.8 0.3 copy.26
  114.0 0.0 copy-start.1
  114.0 0.9 broadcast_in_dim_reshape.6
  114.9 0.3 copy-done.1
  115.3 0.1 copy.27
  115.4 0.3 copy.28
  115.7 0.0 copy-start.4
  115.7 0.9 broadcast_in_dim_reshape.7
  116.6 0.0 copy-done.4
  116.6 0.7 pad_maximum_fusion.1
  (7 shorter events, 0.1 us)
Async XLA Ops:
  0.6 1.4 %copy-start = (s32[1,48,64]{2,1,0:T(8,128)S(1)}, s32[1,48,64]{2,1,0:T(8,128)}, u32[]{:S(2)}) copy-start(s32[1,48,64]{2,1,0:T(8,128)} %param.9) | copy-start | bytes 36868
  0.6 2.2 %copy-start.8 = (bf16[40,1280]{1,0:T(8,128)(2,1)S(1)}, bf16[40,1280]{1,0:T(8,128)(2,1)}, u32[]{:S(2)}) copy-start(bf16[40,1280]{1,0:T(8,128)(2,1)} %param.15) | copy-start | bytes 307204
  2.9 0.9 copy-start.5
  2.9 0.9 copy-start.6
  2.9 1.0 copy-start.7
  2.9 1.8 %copy-start.2 = (bf16[1,3,64,1280]{3,2,1,0:T(8,128)(2,1)S(1)}, bf16[1,3,64,1280]{3,2,1,0:T(8,128)(2,1)}, u32[]{:S(2)}) copy-start(bf16[1,3,64,1280]{3,2,1,0:T(8,128)(2,1)} %param.8) | copy-start | bytes 1474564
  5.0 1.2 %copy-start.3 = (bf16[1,3,64,1280]{3,2,1,0:T(8,128)(2,1)S(1)}, bf16[1,3,64,1280]{3,2,1,0:T(8,128)(2,1)}, u32[]{:S(2)}) copy-start(bf16[1,3,64,1280]{3,2,1,0:T(8,128)(2,1)} %param.10) | copy-start | bytes 1474564
  114.0 1.2 %copy-start.1 = (bf16[16,16,1280]{2,1,0:T(8,128)(2,1)S(1)}, bf16[16,16,1280]{2,1,0:T(8,128)(2,1)}, u32[]{:S(2)}) copy-start(bf16[16,16,1280]{2,1,0:T(8,128)(2,1)} %get-tuple-element.7) | copy-start | bytes 1966084
  115.7 0.9 copy-start.4
